TPU v7x, 256 devices: a whole 4x4x8 slice. The times are simulated.
256 devices in a mesh: prow: 16 (over z, core), pcol: 16 (over y, x).
Axes of the slice: x: 4, y: 4, z: 8, core: 2. Of those that a mesh axis runs over, the one named last changes fastest.
Arguments:
- log_derivs: bfloat16 [512, 16384], P('pcol', 'prow'), may hold values from -12 to 12
- energy_derivs: bfloat16 [512, 16384], P('pcol', 'prow'), may hold values from -6 to 6
- start_block: float32 [16384, 32], P(('prow', 'pcol')), may hold values from -6 to 6
Outputs:
- block_one: float32 [16384, 32], P(('prow', 'pcol'))
- block_two: float32 [16384, 32], P(('prow', 'pcol'))
- rayleigh: float32 [32, 32], replicated
- correlation_tiles: float32 [16, 16384, 1024], P('pcol', 'prow')
- hamiltonian_tiles: float32 [16, 16384, 1024], P('pcol', 'prow')
All inputs are finite; a program needn't handle non-finite values.
Results may differ from a plain program's by a relative error of at most 0.0003.
Values may be sent and summed in bfloat16 or wider, within the bound.
A program may use at most 64 MiB of HBM per device.

v0:
```python
import contextlib
import functools

import jax
import jax.numpy as jnp
from jax import lax
from jax.experimental import pallas as pl
from jax.experimental.pallas import tpu as pltpu
from jax.sharding import PartitionSpec as P

STABILIZER = 0.5
EPSILON = 1e-6
ENLARGED = 2.0**30
F32 = jnp.float32
BF16 = jnp.bfloat16
HIGHEST = lax.Precision.HIGHEST
MESH = pl.DeviceIdType.MESH
NT = (((1,), (1,)), ((), ()))
TN = (((0,), (0,)), ((), ()))


def scope(name):
    return contextlib.nullcontext()


def pieces(x):
    high = x.astype(BF16)
    rest = x - high.astype(F32)
    middle = rest.astype(BF16)
    low = (rest - middle.astype(F32)).astype(BF16)
    return jnp.concatenate([high, middle, low], axis=0)


def sum_rows(x, n):
    return x[:n] + x[n : 2 * n] + x[2 * n : 3 * n]


def to_row(column, eye):
    return jnp.sum(jnp.where(eye, column, 0.0), axis=0, keepdims=True)


def to_column(row, eye):
    return jnp.sum(jnp.where(eye, row, 0.0), axis=1, keepdims=True)


def fold(x):
    return jnp.concatenate([x[8 * g : 8 * g + 8] for g in range(4)], axis=1)


def unfold(folded):
    return jnp.concatenate(
        [
            jnp.concatenate([x[:, 32 * g : 32 * g + 32] for x in folded], axis=1)
            for g in range(4)
        ],
        axis=0,
    )


def inverse_of_two(a, b, d):
    scale = 1.0 / (a * d - b * b)
    return d * scale, -b * scale, a * scale


def solver_of_four(columns, k):
    g = [[columns[j][k + i : k + i + 1] for j in range(4)] for i in range(4)]
    p0, p1, p2 = inverse_of_two(g[0][0], g[1][0], g[1][1])
    t02, t12 = p0 * g[2][0] + p1 * g[2][1], p1 * g[2][0] + p2 * g[2][1]
    t03, t13 = p0 * g[3][0] + p1 * g[3][1], p1 * g[3][0] + p2 * g[3][1]
    w0, w1, w2 = inverse_of_two(
        g[2][2] - g[2][0] * t02 - g[2][1] * t12,
        g[3][2] - g[3][0] * t02 - g[3][1] * t12,
        g[3][3] - g[3][0] * t03 - g[3][1] * t13,
    )

    def solve(array):
        r = [array[k + i : k + i + 1] for i in range(4)]
        u0, u1 = p0 * r[0] + p1 * r[1], p1 * r[0] + p2 * r[1]
        v2 = r[2] - t02 * r[0] - t12 * r[1]
        v3 = r[3] - t03 * r[0] - t13 * r[1]
        x2, x3 = w0 * v2 + w1 * v3, w1 * v2 + w2 * v3
        return u0 - t02 * x2 - t03 * x3, u1 - t12 * x2 - t13 * x3, x2, x3

    return solve


def eliminate(matrix, right, eye):
    n = matrix.shape[0]
    diagonal = jnp.where(eye, matrix, 0.0)
    unit = lax.rsqrt(jnp.sum(diagonal, axis=1, keepdims=True))
    unit_row = lax.rsqrt(jnp.sum(diagonal, axis=0, keepdims=True))
    both = jnp.concatenate([matrix * unit * unit_row, right * unit], axis=1)
    rows = lax.broadcasted_iota(jnp.int32, both.shape, 0)

    def spread(at):
        return [
            jnp.broadcast_to(both[:, at + j : at + j + 1], both.shape)
            for j in range(4 if at < n else 0)
        ]

    now, later = spread(0), spread(4)
    for k in range(0, n, 4):
        solve = solver_of_four(now, k)
        pivots = (rows >= k) & (rows < k + 4)
        c = [
            jnp.where(rows == k + j, -1.0, jnp.where(pivots, 0.0, now[j]))
            for j in range(4)
        ]

        def step(array):
            x = solve(array)
            rest = jnp.where(pivots, 0.0, array)
            return (rest - c[0] * x[0] - c[1] * x[1]) - (c[2] * x[2] + c[3] * x[3])

        now = [step(array) for array in later]
        both = step(both)
        later = spread(k + 8)
    return both[:, n:] * unit


def farthest_first(m, n):
    steps = [(i, j) for i in range(m) for j in range(n) if i or j]
    return sorted(steps, key=lambda s: -min(s[0], m - s[0]) - min(s[1], n - s[1]))


def davidson(
    nr,
    nc,
    l_hbm,
    e_hbm,
    v_hbm,
    tiles_ref,
    one_ref,
    two_ref,
    ray_ref,
    norms_ref,
    l_ref,
    e_ref,
    v_ref,
    block,
    own_t,
    slabs,
    gathered,
    v_send,
    v_recv,
    weights,
    split_all,
    basis,
    pair_send,
    pair_recv,
    image_send,
    image_recv,
    gram_pair_send,
    gram_pair_recv,
    gram_send,
    gram_recv,
    walk_send,
    walk_recv,
    norm_send,
    norm_recv,
    loads,
    sends,
    recvs,
    ring_sems,
):
    p = lax.axis_index("prow")
    q = lax.axis_index("pcol")
    z = p // 2
    core = p % 2
    nz = nr // 2
    wide = 64 * nc
    walkers = 32 * nc
    params = wide * nr

    def row_of(zz, cc):
        return lax.rem(zz + nz, nz) * 2 + cc

    sibling = z * 2 + 1 - core

    def push(src, dst, send_sem, recv_sem, device):
        pltpu.make_async_remote_copy(
            src_ref=src,
            dst_ref=dst,
            send_sem=send_sem,
            recv_sem=recv_sem,
            device_id=device,
            device_id_type=MESH,
        ).start()

    def sent(ref, sem):
        pltpu.make_async_remote_copy(
            src_ref=ref,
            dst_ref=ref,
            send_sem=sem,
            recv_sem=sem,
            device_id={"prow": sibling},
            device_id_type=MESH,
        ).wait_send()

    def landed(ref, sem):
        pltpu.make_async_remote_copy(
            src_ref=ref,
            dst_ref=ref,
            send_sem=sem,
            recv_sem=sem,
            device_id={"prow": sibling},
            device_id_type=MESH,
        ).wait_recv()

    barrier = pltpu.get_barrier_semaphore()

    nx = 4
    ny = nc // nx
    x, y = q % nx, q // nx

    def along_x(i):
        return y * nx + lax.rem(x + i, nx)

    def along_y(i):
        return lax.rem(y + i, ny) * nx + x

    plane = [
        lax.rem(y + j, ny) * nx + lax.rem(x + i, nx)
        for i, j in farthest_first(nx, ny)
    ]
    chips = [row_of(z + i, core) for i, _ in farthest_first(nz, 1)]
    rows = [
        row_of(z + i, lax.rem(core + j, 2)) for i, j in farthest_first(nz, 2)
    ]
    far_rows = len(rows) // 3
    for axis, members in (
        ("pcol", plane[: nc // 3]),
        ("prow", rows[:far_rows]),
        ("pcol", plane[nc // 3 :]),
        ("prow", rows[far_rows:]),
    ):
        for member in members:
            pl.semaphore_signal(
                barrier, inc=1, device_id={axis: member}, device_id_type=MESH
            )
    reads = [
        pltpu.make_async_copy(src, dst, loads.at[i])
        for i, (src, dst) in enumerate(((v_hbm, v_ref), (l_hbm, l_ref), (e_hbm, e_ref)))
    ]
    for read in reads:
        read.start()


    def to_plane(copy):
        for peer in plane:
            copy(peer)

    reads[0].wait()
    v_own = v_ref[...]
    v_send[...] = jnp.concatenate([v_own[:16], v_own[16:]], axis=1)
    v_recv[pl.ds(q, 1)] = v_send[...][None]
    reads[1].wait()
    reads[2].wait()
    l_own = l_ref[...]
    e_own = e_ref[...]
    for j in range(nc):
        slabs[j] = jnp.concatenate(
            [l_own[:, 64 * j : 64 * j + 64], e_own[:, 64 * j : 64 * j + 64]], axis=1
        )
    own_rows = pl.ds(pl.multiple_of(q * 32, 32), 32)
    gathered[pl.ds(p, 1), own_rows, :] = slabs[pl.ds(q, 1)]
    block[own_rows, :] = l_own
    weights[...] = jnp.concatenate([l_own, e_own], axis=0).T
    with scope("barrier"):
        pl.semaphore_wait(barrier, nc - 1 + nr - 1)
    to_plane(
        lambda peer: push(
            v_send, v_recv.at[q], sends.at[0], recvs.at[0], {"pcol": peer}
        )
    )
    def half_of(member, part):
        return block.at[pl.ds(pl.multiple_of(member * 32 + 16 * part, 16), 16)]

    def block_first():
        for i in range(1, nx):
            ref = half_of(q, 0)
            push(ref, ref, sends.at[2], recvs.at[2], {"pcol": along_x(i)})
        for i in range(1, ny):
            ref = half_of(q, 1)
            push(ref, ref, sends.at[10], recvs.at[10], {"pcol": along_y(i)})

    def block_second():
        landed(block.at[pl.ds(0, 16 * (nx - 1))], recvs.at[2])
        landed(block.at[pl.ds(0, 16 * (ny - 1))], recvs.at[10])

        for i, _ in farthest_first(ny, 1):
            for k in range(nx):
                ref = half_of(along_x(k), 0)
                push(ref, ref, sends.at[11], recvs.at[11], {"pcol": along_y(i)})
        for i, _ in farthest_first(nx, 1):
            for k in range(ny):
                ref = half_of(along_y(k), 1)
                push(ref, ref, sends.at[12], recvs.at[12], {"pcol": along_x(i)})

    counts = (nx - 1, ny - 1, nx * (ny - 1), ny * (nx - 1))

    def block_landed():
        for sem, count in zip((11, 12), counts[2:], strict=True):
            landed(block.at[pl.ds(0, 16 * count)], recvs.at[sem])

    def block_sent():
        for sem, count in zip((2, 10, 11, 12), counts, strict=True):
            sent(block.at[pl.ds(0, 16 * count)], sends.at[sem])

    block_first()
    to_plane(
        lambda peer: push(
            slabs.at[peer],
            gathered.at[p, own_rows],
            sends.at[1],
            recvs.at[1],
            {"pcol": peer},
        )
    )

    eye = lax.broadcasted_iota(jnp.int32, (32, 32), 0) == lax.broadcasted_iota(
        jnp.int32, (32, 32), 1
    )
    far = pl.ds(0, nc - 1)

    full = nz // 2 - 1
    half = walkers // 2
    everything, lower, upper = pl.ds(0, walkers), pl.ds(0, half), pl.ds(half, half)

    def part_of(way, step):
        return everything if step < full else (lower, upper)[way]

    def ring_start():
        landed(gathered.at[0, pl.ds(0, 32 * (nc - 1))], recvs.at[1])
        ring_send(0)
        own = gathered.at[p]
        push(
            own,
            own,
            ring_sems.at[2, 0, full + 1],
            ring_sems.at[3, 0, full + 1],
            {"prow": sibling},
        )

    def ring_send(step):
        for way, sign in ((0, 1), (1, -1)):
            ref = gathered.at[row_of(z - sign * step, core), part_of(way, step)]
            push(
                ref,
                ref,
                ring_sems.at[0, way, step],
                ring_sems.at[1, way, step],
                {"prow": row_of(z + sign, core)},
            )

    def ring_landed(step):
        for way, sign in ((0, 1), (1, -1)):
            ref = gathered.at[row_of(z - sign * (step + 1), core), part_of(way, step)]
            landed(ref, ring_sems.at[1, way, step])
            push(
                ref,
                ref,
                ring_sems.at[2, way, step],
                ring_sems.at[3, way, step],
                {"prow": sibling},
            )

    def ring_advance(step):
        if step <= full:
            ring_landed(step)
        if step < full:
            ring_send(step + 1)

    def sibling_landed(step):
        for way, sign in ((0, 1), (1, -1)):
            chunk = row_of(z - sign * (step + 1), 1 - core)
            landed(gathered.at[chunk, part_of(way, step)], ring_sems.at[3, way, step])

    def ring_sent():
        sent(gathered.at[p], ring_sems.at[2, 0, full + 1])
        for step in range(full + 1):
            for way in range(2):
                ref = gathered.at[p, part_of(way, step)]
                sent(ref, ring_sems.at[0, way, step])
                sent(ref, ring_sems.at[2, way, step])

    def multiply(chunk):
        a = gathered[pl.ds(2 * chunk, 1)][0]
        b = gathered[pl.ds(2 * chunk + 1, 1)][0]
        right = jnp.concatenate(
            [a[:, :64], b[:, :64], a[:, 64:], b[:, 64:]], axis=1
        )
        out = jnp.dot(own_t[...], right, preferred_element_type=F32) * (1.0 / walkers)
        columns = pl.ds(pl.multiple_of(chunk * 128, 128), 128)
        tiles_ref[0, :, columns] = out[:, :128]
        tiles_ref[1, :, columns] = out[:, 128:]

    def multiply_own():
        own_t[...] = block[...].T
        landed(gathered.at[sibling], ring_sems.at[3, 0, full + 1])
        multiply(z)
        row = lax.broadcasted_iota(jnp.int32, (64, 128), 0)
        column = lax.broadcasted_iota(jnp.int32, (64, 128), 1)
        mine = pl.ds(pl.multiple_of(q * 64, 64), 64)
        columns = pl.ds(pl.multiple_of(z * 128, 128), 128)
        tiles_ref[0, mine, columns] += jnp.where(
            column == row + core * 64, STABILIZER, 0.0
        )

    def multiply_step(step):
        if step > full:
            return
        sibling_landed(step)

        def body(way, carry):
            multiply(lax.rem(z + (2 * way - 1) * (step + 1) + nz, nz))
            return carry

        lax.fori_loop(0, 2 if step < full else 1, body, 0)

    def both_cores(src, dst, turn, sem):
        push(
            src.at[turn],
            dst.at[turn],
            sends.at[sem + turn],
            recvs.at[sem + turn],
            {"prow": sibling},
        )

    def along_z(src, dst, turn, sem):
        for chip in chips:
            push(
                src.at[turn],
                dst.at[turn, z],
                sends.at[sem + turn],
                recvs.at[sem + turn],
                {"prow": chip},
            )

    def image_start(vec, turn):
        with scope("values"):
            split = pieces(vec)
            out = sum_rows(jnp.dot(split, weights[...], preferred_element_type=F32), 32)
            pair_send[turn] = jnp.concatenate(
                [fold(out[:, :32]), fold(out[:, 32:])], axis=0
            )
        both_cores(pair_send, pair_recv, turn, 4)
        if turn == 0:
            with scope("block_second"):
                block_second()
        with scope("wait_pair"):
            landed(pair_recv.at[turn], recvs.at[4 + turn])
        with scope("pair_sum"):
            mine = pair_send[turn] + pair_recv[turn]
            image_send[turn] = mine
            image_recv[turn, pl.ds(z, 1)] = mine[None]
        along_z(image_send, image_recv, turn, 6)
        if turn == 1:
            sent(v_recv.at[far], sends.at[0])
        with scope("gram"):
            split_all[...] = split
            out = lax.dot_general(
                split, split_all[...], NT, preferred_element_type=F32
            )
            out = sum_rows(out, 32)
            gram_pair_send[turn] = fold(out[:, :32] + out[:, 32:64] + out[:, 64:])
        both_cores(gram_pair_send, gram_pair_recv, turn, 15)

    def gram_start(turn):
        landed(gram_pair_recv.at[turn], recvs.at[15 + turn])
        mine = gram_pair_send[turn] + gram_pair_recv[turn]
        gram_send[turn] = mine
        gram_recv[turn, pl.ds(z, 1)] = mine[None]
        along_z(gram_send, gram_recv, turn, 13)

    def walk_start(turn):
        with scope("wait_image"):
            landed(image_recv.at[turn, pl.ds(0, nz - 1)], recvs.at[6 + turn])
        with scope("image_sum"):
            mine = jnp.sum(image_recv[turn], axis=0)
            walk_send[turn] = mine
        walk_recv[turn, pl.ds(q, 1)] = mine[None]
        to_plane(
            lambda peer: push(
                walk_send.at[turn],
                walk_recv.at[turn, q],
                sends.at[8 + turn],
                recvs.at[8 + turn],
                {"pcol": peer},
            )
        )

    def gram_landed(turn):
        landed(gram_recv.at[turn, pl.ds(0, nz - 1)], recvs.at[13 + turn])
        return unfold([jnp.sum(gram_recv[turn], axis=0)])

    def walk_landed(turn):
        with scope("wait_walk"):
            landed(walk_recv.at[turn, far], recvs.at[8 + turn])
        return [
            jnp.concatenate(
                [
                    unfold([walk_recv[turn, k + j, rows] for j in range(4)])
                    for k in range(0, nc, 4)
                ],
                axis=1,
            )
            for rows in (slice(0, 8), slice(8, 16))
        ]

    def residual(vec, l_val, e_val, gram, inverse_diag):
        with scope("products"):
            l_split = pieces(l_val)
            both = jnp.concatenate([l_split, pieces(e_val)], axis=0)
            out = sum_rows(
                lax.dot_general(l_split, both, NT, preferred_element_type=F32), 32
            )
        ray_s = out[:, :32] + out[:, 32:64] + out[:, 64:96]
        ray_h = out[:, 96:128] + out[:, 128:160] + out[:, 160:192]
        with scope("images"):
            image = jnp.dot(both, block[...], preferred_element_type=F32)
            image_s = sum_rows(image[:96], 32) * (1.0 / walkers) + STABILIZER * vec
            image_h = sum_rows(image[96:], 32) * (1.0 / walkers) * inverse_diag
            s = pieces(image_s * inverse_diag)
            right = jnp.concatenate(
                [s[:32], s[32:64], s[:32], s[64:], s[32:64], s[:32]], axis=0
            )
        with scope("eliminate"):
            coeffs = eliminate(
                ray_s * (1.0 / walkers) + STABILIZER * gram,
                ray_h * (1.0 / walkers),
                eye,
            )
        with scope("mix"):
            c = pieces(coeffs)
            left = jnp.concatenate(
                [c[:32], c[:32], c[32:64], c[:32], c[32:64], c[64:]], axis=0
            )
            out = lax.dot_general(left, right, TN, preferred_element_type=F32)
            result = image_h - out
        return result, coeffs

    def own_part(vec):
        for k in range(nc // 2):
            basis[k] = vec[:, 128 * k : 128 * k + 128]
        chunk = basis[pl.ds(q // 2, 1)][0]
        return jnp.where(q % 2 == 0, chunk[:, :64], chunk[:, 64:])

    with scope("wait_v"):
        landed(v_recv.at[far], recvs.at[0])
    top, bottom = [], []
    for k in range(0, nc, 2):
        a, b = v_recv[k], v_recv[k + 1]
        top += [a[:, :64], b[:, :64]]
        bottom += [a[:, 64:], b[:, 64:]]
    vec = jnp.concatenate(
        [jnp.concatenate(top, axis=1), jnp.concatenate(bottom, axis=1)], axis=0
    )
    image_start(vec, 0)
    with scope("ring_start"):
        ring_start()
    gram_start(0)
    walk_start(0)
    with scope("wait_block"):
        block_landed()
    squares = jnp.zeros((8, wide), F32)
    for k in range(0, walkers, 16):
        part = block[k : k + 16].astype(F32)
        part = part * part
        squares = squares + part[:8] + part[8:]
    inverse_diag = 1.0 / (
        jnp.sum(squares, axis=0, keepdims=True) * (1.0 / walkers) + STABILIZER
    )
    gram = gram_landed(0)
    with scope("ring_0"):
        ring_advance(0)
    l_val, e_val = walk_landed(0)
    vec, _ = residual(vec, l_val, e_val, gram, inverse_diag * ENLARGED)

    image_start(vec, 1)
    with scope("ring_1"):
        ring_advance(1)
    gram_start(1)
    with scope("tiles_a"):
        multiply_own()
    walk_start(1)
    with scope("tiles_b"):
        multiply_step(0)
    with scope("ring_2"):
        ring_advance(2)
    gram = gram_landed(1)
    norms = jnp.sum(jnp.where(eye, gram, 0.0), axis=1, keepdims=True)
    norms = norms * (1.0 / ENLARGED) * (1.0 / ENLARGED)
    scale = (1.0 / ENLARGED) / jnp.sqrt(norms * (1.0 / params) + EPSILON)
    gram = gram * scale * to_row(scale, eye)
    vec = vec * scale
    one_ref[...] = own_part(vec)
    l_val, e_val = walk_landed(1)
    vec, coeffs = residual(vec, l_val * scale, e_val * scale, gram, inverse_diag)
    norms = to_row(jnp.sum(vec * vec, axis=1, keepdims=True), eye)
    norm_send[...] = jnp.concatenate([norms, jnp.zeros((1, 96), F32)], axis=1)
    norm_recv[pl.ds(p, 1)] = norm_send[...][None]

    for row in rows:
        push(norm_send, norm_recv.at[p], sends.at[3], recvs.at[3], {"prow": row})
    block_sent()
    ray_ref[...] = coeffs
    two_ref[...] = own_part(vec)
    with scope("tiles_c"):
        multiply_step(1)
        multiply_step(2)
    with scope("ring_3"):
        ring_advance(3)
    with scope("tiles_d"):
        multiply_step(3)
    ring_sent()
    sent(gathered.at[0, pl.ds(0, 32 * (nc - 1))], sends.at[1])
    for turn in range(2):
        sent(pair_send.at[turn], sends.at[4 + turn])
        sent(gram_pair_send.at[turn], sends.at[15 + turn])
        sent(image_recv.at[turn, pl.ds(0, nz - 1)], sends.at[6 + turn])
        sent(gram_recv.at[turn, pl.ds(0, nz - 1)], sends.at[13 + turn])
        sent(walk_recv.at[turn, far], sends.at[8 + turn])
    with scope("wait_norm"):
        landed(norm_recv.at[pl.ds(0, nr - 1)], recvs.at[3])
    norms_ref[...] = jnp.sum(norm_recv[...], axis=0)
    sent(norm_recv.at[pl.ds(0, nr - 1)], sends.at[3])


def write(
    params,
    tiles,
    one,
    two,
    ray,
    norms,
    corr_ref,
    ham_ref,
    one_ref,
    two_ref,
    ray_ref,
    scaled,
    sems,
):
    rows = tiles.shape[1] // 4
    pairs = []
    for k in range(4):
        part = pl.ds(k * rows, rows)
        pairs.append((tiles.at[0, part], corr_ref.at[0, part]))
        pairs.append((tiles.at[1, part], ham_ref.at[0, part]))
    pairs += [(one, one_ref), (ray, ray_ref), (scaled, two_ref)]
    writes = [
        pltpu.make_async_copy(src, dst, sems.at[i])
        for i, (src, dst) in enumerate(pairs)
    ]
    for copy in writes[:-1]:
        copy.start()
    eye = lax.broadcasted_iota(jnp.int32, (32, 32), 0) == lax.broadcasted_iota(
        jnp.int32, (32, 32), 1
    )
    squares = to_column(norms[:, :32], eye)
    scaled[...] = two[...] * (1.0 / jnp.sqrt(squares * (1.0 / params) + EPSILON))
    writes[-1].start()
    for copy in writes:
        copy.wait()


def local(nr, nc, log_derivs, energy_derivs, start_block):
    wide, walkers, narrow = 64 * nc, 32 * nc, 64 * nr
    nz = nr // 2
    vmem = pl.BlockSpec(memory_space=pltpu.VMEM)
    full = nz // 2 - 1
    hbm = pl.BlockSpec(memory_space=pltpu.HBM)
    small = (
        jax.ShapeDtypeStruct((32, 64), F32),
        jax.ShapeDtypeStruct((32, 64), F32),
        jax.ShapeDtypeStruct((32, 32), F32),
    )
    arguments = (log_derivs, energy_derivs, start_block.T)
    results = pl.pallas_call(
        functools.partial(davidson, nr, nc),
        out_shape=(
            pltpu.VMEM((2, wide, narrow), F32),
            *(pltpu.VMEM(x.shape, F32) for x in small),
            pltpu.VMEM((1, 128), F32),
        ),
        in_specs=[hbm] * 3,
        out_specs=(vmem,) * 5,
        scratch_shapes=[
            pltpu.VMEM((32, wide), BF16),
            pltpu.VMEM((32, wide), BF16),
            pltpu.VMEM((32, 64), F32),
            pltpu.VMEM((walkers, wide), BF16),
            pltpu.VMEM((wide, walkers), BF16),
            pltpu.VMEM((nc, 32, 128), BF16),
            pltpu.VMEM((nr, walkers, 128), BF16),
            pltpu.VMEM((16, 128), F32),
            pltpu.VMEM((nc, 16, 128), F32),
            pltpu.VMEM((wide, 64), BF16),
            pltpu.VMEM((96, wide), BF16),
            pltpu.VMEM((nc // 2, 32, 128), F32),
            pltpu.VMEM((2, 16, 128), F32),
            pltpu.VMEM((2, 16, 128), F32),
            pltpu.VMEM((2, 16, 128), F32),
            pltpu.VMEM((2, nz, 16, 128), F32),
            pltpu.VMEM((2, 8, 128), F32),
            pltpu.VMEM((2, 8, 128), F32),
            pltpu.VMEM((2, 8, 128), F32),
            pltpu.VMEM((2, nz, 8, 128), F32),
            pltpu.VMEM((2, 16, 128), F32),
            pltpu.VMEM((2, nc, 16, 128), F32),
            pltpu.VMEM((1, 128), F32),
            pltpu.VMEM((nr, 1, 128), F32),
            pltpu.SemaphoreType.DMA((3,)),
            pltpu.SemaphoreType.DMA((17,)),
            pltpu.SemaphoreType.DMA((17,)),
            pltpu.SemaphoreType.DMA((4, 2, full + 2)),
        ],
        compiler_params=pltpu.CompilerParams(
            collective_id=0, has_side_effects=True, vmem_limit_bytes=24 * 1024 * 1024
        ),
        name="davidson",
    )(*(pltpu.with_memory_space_constraint(x, pltpu.HBM) for x in arguments))

    corr, ham, one, two, ray = pl.pallas_call(
        functools.partial(write, 64 * nc * nr),
        out_shape=(
            jax.ShapeDtypeStruct((1, wide, narrow), F32),
            jax.ShapeDtypeStruct((1, wide, narrow), F32),
            *small,
        ),
        in_specs=[vmem] * 5,
        out_specs=(hbm,) * 5,
        scratch_shapes=[pltpu.VMEM((32, 64), F32), pltpu.SemaphoreType.DMA((11,))],
        compiler_params=pltpu.CompilerParams(vmem_limit_bytes=24 * 1024 * 1024),
        name="tiles",
    )(*(pltpu.with_memory_space_constraint(x, pltpu.VMEM) for x in results))
    return one.T, two.T, ray, corr, ham


def solution(mesh):
    return jax.shard_map(
        functools.partial(local, mesh.shape["prow"], mesh.shape["pcol"]),
        mesh=mesh,
        in_specs=(P("pcol", "prow"), P("pcol", "prow"), P(("prow", "pcol"), None)),
        out_specs=(
            P(("prow", "pcol"), None),
            P(("prow", "pcol"), None),
            P(),
            P("pcol", "prow", None),
            P("pcol", "prow", None),
        ),
        check_vma=False,
    )
```

profile of v0, /device:TPU:1, one launch (start us, length us, event | category | flops | bytes accessed | tf_op | source)
XLA Modules:
  0.0 48.8 jit_solution(6639386349852417179)
XLA Ops:
  0.6 44.8 %davidson.1 = (f32[2,1024,1024]{2,1,0:T(8,128)S(1)}, f32[32,64]{1,0:T(8,128)S(1)}, f32[32,64]{1,0:T(8,128)S(1)}, f32[32,32]{1,0:T(8,128)S(1)}, f32[1,128]{1,0:T(1,128)S(1)}) custom-call(bf16[32,1024]{1,0:T(8,128)(2,1)} %l_hbm.1, bf16[32,1024]{1,0:T(8,128)(2,1)} %e_hbm.1, f32[32,64]{1,0:T(8,128)} %bitcast.3), custom_call_target="tpu_custom_call" | custom-call | tf_op jit(solution)/shard_map/davidson/pallas_call | solution.py:680
  45.4 3.4 %tiles.1 = (f32[1,1024,1024]{2,1,0:T(8,128)}, f32[1,1024,1024]{2,1,0:T(8,128)}, f32[32,64]{1,0:T(8,128)}, f32[32,64]{1,0:T(8,128)}, f32[32,32]{1,0:T(8,128)}) custom-call(f32[2,1024,1024]{2,1,0:T(8,128)S(1)} %get-tuple-element.15.tiles, f32[32,64]{1,0:T(8,128)S(1)} %get-tuple-element.16.one, f32[32,64]{1,0:T(8,128)S(1)} %get-tuple-element.17.two, ...), custom_call_target="tpu_custom_call" | custom-call | tf_op jit(solution)/shard_map/tiles/pallas_call | solution.py:725
where the time goes:
time: 49 us; the launch traced here: 48.8 us
  Pallas kernels  48.2 us (98%)
  between operations  0.64 us (1%)
    pallas_call x1, Pallas kernels, local(): pl.pallas_call(functools.partial(davidson, nr, nc), out_shape=(pltpu.VMEM...  44.8 us
    pallas_call x1, Pallas kernels, local(): pl.pallas_call(functools.partial(write, 64 * nc * nr), out_shape=(jax.Sha...  3.4 us

commit v1 on v0

--- a/solution.py
+++ b/solution.py
@@ -578,16 +578,14 @@
     vec, _ = residual(vec, l_val, e_val, gram, inverse_diag * ENLARGED)
 
     image_start(vec, 1)
+    gram_start(1)
     with scope("ring_1"):
         ring_advance(1)
-    gram_start(1)
     with scope("tiles_a"):
         multiply_own()
     walk_start(1)
     with scope("tiles_b"):
         multiply_step(0)
-    with scope("ring_2"):
-        ring_advance(2)
     gram = gram_landed(1)
     norms = jnp.sum(jnp.where(eye, gram, 0.0), axis=1, keepdims=True)
     norms = norms * (1.0 / ENLARGED) * (1.0 / ENLARGED)
@@ -595,6 +593,8 @@
     gram = gram * scale * to_row(scale, eye)
     vec = vec * scale
     one_ref[...] = own_part(vec)
+    with scope("ring_2"):
+        ring_advance(2)
     l_val, e_val = walk_landed(1)
     vec, coeffs = residual(vec, l_val * scale, e_val * scale, gram, inverse_diag)
     norms = to_row(jnp.sum(vec * vec, axis=1, keepdims=True), eye)

time: 49 us -> 49 us (level)
  no operation moved by 1% of the time
where the time goes in v1:
time: 49 us; the launch traced here: 48.9 us
  Pallas kernels  48.2 us (98%)
  between operations  0.64 us (1%)
    pallas_call x1, Pallas kernels, local(): pl.pallas_call(functools.partial(davidson, nr, nc), out_shape=(pltpu.VMEM...  44.8 us
    pallas_call x1, Pallas kernels, local(): pl.pallas_call(functools.partial(write, 64 * nc * nr), out_shape=(jax.Sha...  3.4 us

profile of v1, /device:TPU:1, one launch (start us, length us, event | category | flops | bytes accessed | tf_op | source)
XLA Modules:
  0.0 48.9 jit_solution(9390188718506419132)
XLA Ops:
  0.6 44.8 %davidson.1 = (f32[2,1024,1024]{2,1,0:T(8,128)S(1)}, f32[32,64]{1,0:T(8,128)S(1)}, f32[32,64]{1,0:T(8,128)S(1)}, f32[32,32]{1,0:T(8,128)S(1)}, f32[1,128]{1,0:T(1,128)S(1)}) custom-call(bf16[32,1024]{1,0:T(8,128)(2,1)} %l_hbm.1, bf16[32,1024]{1,0:T(8,128)(2,1)} %e_hbm.1, f32[32,64]{1,0:T(8,128)} %bitcast.3), custom_call_target="tpu_custom_call" | custom-call | tf_op jit(solution)/shard_map/davidson/pallas_call | solution.py:680
  45.5 3.4 %tiles.1 = (f32[1,1024,1024]{2,1,0:T(8,128)}, f32[1,1024,1024]{2,1,0:T(8,128)}, f32[32,64]{1,0:T(8,128)}, f32[32,64]{1,0:T(8,128)}, f32[32,32]{1,0:T(8,128)}) custom-call(f32[2,1024,1024]{2,1,0:T(8,128)S(1)} %get-tuple-element.15.tiles, f32[32,64]{1,0:T(8,128)S(1)} %get-tuple-element.16.one, f32[32,64]{1,0:T(8,128)S(1)} %get-tuple-element.17.two, ...), custom_call_target="tpu_custom_call" | custom-call | tf_op jit(solution)/shard_map/tiles/pallas_call | solution.py:725

commit v2 on v1

--- a/solution.py
+++ b/solution.py
@@ -592,7 +592,7 @@
     scale = (1.0 / ENLARGED) / jnp.sqrt(norms * (1.0 / params) + EPSILON)
     gram = gram * scale * to_row(scale, eye)
     vec = vec * scale
-    one_ref[...] = own_part(vec)
+    first_block = vec
     with scope("ring_2"):
         ring_advance(2)
     l_val, e_val = walk_landed(1)
@@ -606,6 +606,7 @@
     block_sent()
     ray_ref[...] = coeffs
     two_ref[...] = own_part(vec)
+    one_ref[...] = own_part(first_block)
     with scope("tiles_c"):
         multiply_step(1)
         multiply_step(2)

time: 49 us -> 49.1 us (level)
  no operation moved by 1% of the time
where the time goes in v2:
time: 49.1 us; the launch traced here: 48.9 us
  Pallas kernels  48.2 us (98%)
  between operations  0.64 us (1%)
    pallas_call x1, Pallas kernels, local(): pl.pallas_call(functools.partial(davidson, nr, nc), out_shape=(pltpu.VMEM...  44.8 us
    pallas_call x1, Pallas kernels, local(): pl.pallas_call(functools.partial(write, 64 * nc * nr), out_shape=(jax.Sha...  3.4 us

profile of v2, /device:TPU:1, one launch (start us, length us, event | category | flops | bytes accessed | tf_op | source)
XLA Modules:
  0.0 48.9 jit_solution(15663873279573143440)
XLA Ops:
  0.6 44.8 %davidson.1 = (f32[2,1024,1024]{2,1,0:T(8,128)S(1)}, f32[32,64]{1,0:T(8,128)S(1)}, f32[32,64]{1,0:T(8,128)S(1)}, f32[32,32]{1,0:T(8,128)S(1)}, f32[1,128]{1,0:T(1,128)S(1)}) custom-call(bf16[32,1024]{1,0:T(8,128)(2,1)} %l_hbm.1, bf16[32,1024]{1,0:T(8,128)(2,1)} %e_hbm.1, f32[32,64]{1,0:T(8,128)} %bitcast.3), custom_call_target="tpu_custom_call" | custom-call | tf_op jit(solution)/shard_map/davidson/pallas_call | solution.py:681
  45.5 3.4 %tiles.1 = (f32[1,1024,1024]{2,1,0:T(8,128)}, f32[1,1024,1024]{2,1,0:T(8,128)}, f32[32,64]{1,0:T(8,128)}, f32[32,64]{1,0:T(8,128)}, f32[32,32]{1,0:T(8,128)}) custom-call(f32[2,1024,1024]{2,1,0:T(8,128)S(1)} %get-tuple-element.15.tiles, f32[32,64]{1,0:T(8,128)S(1)} %get-tuple-element.16.one, f32[32,64]{1,0:T(8,128)S(1)} %get-tuple-element.17.two, ...), custom_call_target="tpu_custom_call" | custom-call | tf_op jit(solution)/shard_map/tiles/pallas_call | solution.py:726
